TPU v7x, 1024 devices: a whole 4x8x16 slice. The times are simulated.
1024 devices in a mesh: clus: 128 (over z, y), rhs: 8 (over x, core).
Axes of the slice: x: 4, y: 8, z: 16, core: 2. Of those that a mesh axis runs over, the one named last changes fastest.
Arguments:
- points: float32 [3, 262144], P(None, 'clus'), may hold values from 0 to 1
- rhs_cols: float32 [32, 262144], P('rhs', 'clus'), may hold values from -6 to 6
- leaf_basis: float32 [1024, 64, 256], P('clus', 'rhs'), may hold values from -0.375 to 0.375
- leaf_nodes: float32 [1024, 3, 64], P('clus'), may hold values from 0 to 1
- leaf_transfer: float32 [1024, 64, 64], P('clus'), may hold values from -0.25 to 0.25
- near_mask: int32 [1024, 9], P('clus'), may hold values 0 or 1
- top_transfer: float32 [252, 64, 64], replicated, may hold values from -0.5 to 0.5
- top_nodes: float32 [254, 3, 64], replicated, may hold values from 0 to 1
Outputs:
- product: float32 [32, 262144], P('rhs', 'clus')
All inputs are finite; a program needn't handle non-finite values. No bound on the sum of `near_mask` on one device may be relied on, other than what follows from the above.
Results may differ from a plain program's by a relative error of at most 0.0003.
Values sent between devices are 32-bit elements; how exact they have to be, the bound alone decides.
A program may use at most 64 MiB of HBM per device.

v0:
```python
import jax
import jax.numpy as jnp
from jax import lax
from jax.sharding import PartitionSpec as P

AMPLITUDE = 0.2
INV_SCALE = 1.0 / (2.0 * 0.15 * 0.15)
HIGHEST = lax.Precision.HIGHEST


def with_halo(cells, sides, width):
    for axis, dim in sides:
        count = lax.axis_size(axis)
        ends = count - 1
        head = lax.slice_in_dim(cells, 0, width, axis=dim)
        tail = lax.slice_in_dim(cells, cells.shape[dim] - width, cells.shape[dim], axis=dim)
        cells = jnp.concatenate(
            [
                lax.ppermute(tail, axis, [(i, (i + 1) % count) for i in range(ends)]),
                cells,
                lax.ppermute(head, axis, [((i + 1) % count, i) for i in range(ends)]),
            ],
            axis=dim,
        )
    return cells


def kernel_block(targets, sources):
    first = targets[..., 0, :, None] - sources[..., 0, None, :]
    second = targets[..., 1, :, None] - sources[..., 1, None, :]
    third = targets[..., 2, :, None] - sources[..., 2, None, :]
    dist = first * first + second * second + third * third
    return AMPLITUDE * jnp.exp(-dist * INV_SCALE)


def matvec(matrix, vector):
    return jnp.dot(matrix, vector, precision=HIGHEST)


def near_leaves(indices, points, win_points, win_rhs, column_weights, leaf, slots):

    def near_leaf(index):
        start = index * leaf
        window_points = lax.dynamic_slice_in_dim(win_points, start, slots * leaf, 1)
        window_rhs = lax.dynamic_slice_in_dim(win_rhs, start, slots * leaf, 1)
        own = lax.dynamic_slice_in_dim(points, start, leaf, 1)
        block = kernel_block(own, window_points) * column_weights[index][None, :]
        return jnp.dot(window_rhs, block.T, precision=HIGHEST)

    return lax.map(near_leaf, indices)


def on_device(
    points, rhs_cols, leaf_basis, leaf_nodes, leaf_transfer, near_mask, top_transfer, top_nodes
):
    leaves = leaf_nodes.shape[0]
    rank = leaf_nodes.shape[2]
    leaf = leaf_basis.shape[2]
    columns = rhs_cols.shape[0]
    slots = near_mask.shape[1]
    reach = (slots - 1) // 2
    basis = lax.all_gather(leaf_basis, "rhs", axis=1, tiled=True)
    rhs_leaf = rhs_cols.reshape(columns, leaves, leaf)
    moments = jnp.einsum("grl,cgl->grc", basis, rhs_leaf, precision=HIGHEST)
    packed = jnp.concatenate([jnp.transpose(moments, (0, 2, 1)), leaf_nodes], axis=1)
    wide_far = with_halo(packed, (("clus", 0),), reach)
    stacked = jnp.concatenate([points, rhs_cols], axis=0)
    wide_near = with_halo(stacked, (("clus", 1),), reach * leaf)
    slot_ids = jnp.arange(slots, dtype=jnp.int32)
    weights = jnp.where(slot_ids[None, :] == reach, 1, near_mask).astype(jnp.float32)
    column_weights = jnp.repeat(weights, leaf, axis=1)
    near = near_leaves(
        jnp.arange(leaves, dtype=jnp.int32),
        points,
        wide_near[:3],
        wide_near[3:],
        column_weights,
        leaf,
        slots,
    )
    local_far = jnp.zeros((leaves, rank, columns), jnp.float32)
    for slot in range(slots):
        source = wide_far[slot : slot + leaves]
        coupling = kernel_block(leaf_nodes, source[:, columns:, :])
        term = jnp.einsum("gab,gcb->gac", coupling, source[:, :columns, :], precision=HIGHEST)
        local_far = local_far + (1.0 - weights[:, slot])[:, None, None] * term
    lifted = jnp.einsum("gab,gbc->gac", leaf_transfer, moments, precision=HIGHEST)
    root = jnp.sum(lifted, axis=0)
    devices = lax.axis_size("clus")
    levels = devices.bit_length() - 1
    mine = lax.axis_index("clus")
    couples = []
    everyone = lax.all_gather(root[None], "clus", axis=0, tiled=True)
    upward = [everyone]
    for level in range(levels - 1):
        count = devices >> level
        offset = 2 * devices - 2 * count
        terms = jnp.einsum(
            "nab,nbc->nac", top_transfer[offset : offset + count], upward[level], precision=HIGHEST
        )
        upward.append(terms[0::2] + terms[1::2])
    for level in range(levels):
        count = devices >> level
        offset = 2 * devices - 2 * count
        node = mine >> level
        partner = node ^ 1
        partner_moment = lax.dynamic_index_in_dim(upward[level], partner, 0, keepdims=False)
        own_nodes = lax.dynamic_index_in_dim(top_nodes, offset + node, 0, keepdims=False)
        partner_nodes = lax.dynamic_index_in_dim(top_nodes, offset + partner, 0, keepdims=False)
        couples.append(matvec(kernel_block(own_nodes, partner_nodes), partner_moment))
    downward = couples[levels - 1]
    for level in range(levels - 2, -1, -1):
        count = devices >> level
        offset = 2 * devices - 2 * count
        node = mine >> level
        transfer = lax.dynamic_index_in_dim(top_transfer, offset + node, 0, keepdims=False)
        downward = couples[level] + jnp.dot(transfer.T, downward, precision=HIGHEST)
    local = local_far + jnp.einsum("gba,bc->gac", leaf_transfer, downward, precision=HIGHEST)
    far = jnp.einsum("grl,grc->cgl", basis, local, precision=HIGHEST)
    product = jnp.transpose(near, (1, 0, 2)) + far
    return product.reshape(columns, leaves * leaf)


def solution(mesh):
    return jax.shard_map(
        on_device,
        mesh=mesh,
        in_specs=(
            P(None, "clus"),
            P("rhs", "clus"),
            P("clus", "rhs", None),
            P("clus", None, None),
            P("clus", None, None),
            P("clus", None),
            P(),
            P(),
        ),
        out_specs=P("rhs", "clus"),
        check_vma=False,
    )
```

profile of v0, /device:TPU:2, one launch (start us, length us, event | category | flops | bytes accessed | tf_op | source)
XLA Modules:
  0.0 286.7 jit_solution(16045074655163151036)
XLA Ops:
  1.4 4.1 %collective-permute-start = (f32[7,1024]{1,0:T(8,128)}, f32[7,1024]{1,0:T(8,128)}, u32[]{:S(2)}, u32[]{:S(2)}) collective-permute-start(f32[7,1024]{1,0:T(8,128)} %get-tuple-element.121), channel_id=1, source_target_pairs={{0,8},{8,16},{16,24},{24,32},{32,40},{40,48},{48,56},{56,64},{64,7... | collective-permute-start | bytes 86024 | tf_op jit(solution)/shard_map/ppermute | solution.py:19
  7.5 21.2 %all_gather.6 = f32[8,64,256]{2,1,0:T(8,128)S(1)} all-gather(f32[8,8,256]{2,1,0:T(8,128)} %param.12), channel_id=1, replica_groups=mesh['clus'=128,'rhs'=8] {'rhs'}, dimensions={1}, use_global_device_ids=true | all-gather | bytes 589824 | tf_op jit(solution)/shard_map/all_gather | solution.py:62
  32.0 5.8 %collective-permute-start.2 = (f32[4,7,64]{2,1,0:T(8,128)}, f32[4,7,64]{2,1,0:T(8,128)}, u32[]{:S(2)}, u32[]{:S(2)}) collective-permute-start(f32[4,7,64]{2,1,0:T(8,128)} %get-tuple-element.150), channel_id=1, source_target_pairs={{0,8},{8,16},{16,24},{24,32},{32,40},{40,48},{48,56},{56,64},{64,7... | collective-permute-start | bytes 21512 | tf_op jit(solution)/shard_map/ppermute | solution.py:19
  40.0 3.5 %slice.561 = f32[32,64,64]{0,2,1:T(8,128)} slice(f32[252,64,64]{0,2,1:T(8,128)} %param.16), slice={[192:224], [0:64], [0:64]} | slice | bytes 1048576 | tf_op jit(solution)/shard_map/slice | solution.py:99
  49.6 107.0 %all-gather.1 = f32[128,64,4]{1,2,0:T(4,128)S(1)} all-gather(f32[1,64,4]{1,2,0:T(4,128)S(1)} %convolution_bitcast_fusion.7), channel_id=2, replica_groups=mesh['clus'=128,'rhs'=8] {'clus'}, dimensions={0}, use_global_device_ids=true | all-gather | bytes 132096 | tf_op jit(solution)/shard_map/all_gather | solution.py:93
  156.6 3.6 %copy.53 = f32[32,64,64]{2,1,0:T(8,128)} copy(f32[32,64,64]{0,2,1:T(8,128)} %slice.561) | data formatting | bytes 1048576
  160.2 3.0 %copy.55 = f32[16,64,64]{2,1,0:T(8,128)} copy(f32[16,64,64]{0,2,1:T(8,128)} %slice.570) | data formatting | bytes 524288
  163.2 2.7 copy.51
  166.0 3.0 %copy.57 = f32[8,64,64]{2,1,0:T(8,128)} copy(f32[8,64,64]{0,2,1:T(8,128)} %slice.579) | data formatting | bytes 262144
  169.0 4.5 %copy.49 = f32[128,64,64]{2,1,0:T(8,128)} copy(f32[128,64,64]{0,2,1:T(8,128)S(1)} %slice-done.1) | data formatting | bytes 4194304
  173.5 8.6 %convolution_bitcast_fusion = f32[128,64,4]{1,2,0:T(4,128)S(1)} fusion(f32[128,64,4]{1,2,0:T(4,128)S(1)} %all-gather.1, f32[128,64,64]{2,1,0:T(8,128)} %copy.49), kind=kOutput, calls=%fused_computation.31 | convolution fusion | flops 25165824 | bytes 2359296 | tf_op jit(solution)/shard_map/nab,nbc->nac/dot_general | solution.py:98
  182.3 3.4 %convolution_bitcast_fusion.1 = f32[64,64,4]{1,2,0:T(4,128)S(1)} fusion(f32[64,64,4]{1,2,0:T(4,128)S(1)} %slice_add_fusion, f32[64,64,64]{2,1,0:T(8,128)S(1)} %copy-done.4), kind=kOutput, calls=%fused_computation.32 | convolution fusion | flops 12582912 | bytes 1179648 | tf_op jit(solution)/shard_map/nab,nbc->nac/dot_general | solution.py:98
  190.6 12.0 %constant_dynamic-slice_fusion.13 = (f32[1,64,64]{0,2,1:T(8,128)}, f32[1,64,64]{0,2,1:T(8,128)}, f32[1,64,64]{0,2,1:T(8,128)}, f32[1,64,64]{0,2,1:T(8,128)}, f32[1,64,64]{0,2,1:T(8,128)}, /*index=5*/f32[1,64,64]{0,2,1:T(8,128)S(1)}) fusion(f32[252,64,64]{0,2,1:T(8,128)} %param.16, s32[]{:T(128)S(6)} %select_n.108, s32[]{:T(128)S(6)} %select_n.128, ...), kind=kLoop, calls=%fused_computation.475 | loop fusion | bytes 196632 | tf_op jit(solution)/shard_map/jit(dynamic_index_in_dim)/dynamic_slice | solution.py:116
  202.7 2.9 %copy.48 = f32[1,64,64]{2,1,0:T(8,128)} copy(f32[1,64,64]{0,2,1:T(8,128)} %get-tuple-element.115) | data formatting | bytes 32768
  205.6 2.9 %copy.58 = f32[1,64,64]{2,1,0:T(8,128)} copy(f32[1,64,64]{0,2,1:T(8,128)} %get-tuple-element.116) | data formatting | bytes 32768
  208.4 2.9 %copy.56 = f32[1,64,64]{2,1,0:T(8,128)} copy(f32[1,64,64]{0,2,1:T(8,128)} %get-tuple-element.117) | data formatting | bytes 32768
  211.3 2.9 %copy.54 = f32[1,64,64]{2,1,0:T(8,128)} copy(f32[1,64,64]{0,2,1:T(8,128)} %get-tuple-element.118) | data formatting | bytes 32768
  214.2 2.9 %copy.52 = f32[1,64,64]{2,1,0:T(8,128)} copy(f32[1,64,64]{0,2,1:T(8,128)} %get-tuple-element.119) | data formatting | bytes 32768
  237.6 48.1 %while.10 = (s32[]{:T(128)}, f32[8,4,256]{2,1,0:T(4,128)S(1)}, s32[8]{0:T(128)S(1)}, f32[4,4096]{1,0:T(4,128)S(1)}, f32[3,2048]{1,0:T(4,128)S(1)}, /*index=5*/f3...) while((s32[]{:T(128)}, f32[8,4,256]{2,1,0:T(4,128)S(1)}, ...), condition=%wide.region_1.2_spmd, body=%wide.region_0.1_spmd.sunk | while | flops 34801932 | bytes 173382 | solution.py:50
  247.0 2.6 fusion.466
  253.0 2.6 fusion.466
  259.0 2.6 fusion.466
  271.1 2.6 fusion.466
  277.1 2.6 fusion.466
  (138 shorter events, 55.4 us)
Async XLA Ops:
  0.0 49.3 %copy-start = (f32[8,64,64]{2,1,0:T(8,128)S(1)}, f32[8,64,64]{2,1,0:T(8,128)}, u32[]{:S(2)}) copy-start(f32[8,64,64]{2,1,0:T(8,128)} %param.14) | copy-start | bytes 393220
  1.4 235.2 %collective-permute-start = (f32[7,1024]{1,0:T(8,128)}, f32[7,1024]{1,0:T(8,128)}, u32[]{:S(2)}, u32[]{:S(2)}) collective-permute-start(f32[7,1024]{1,0:T(8,128)} %get-tuple-element.121), channel_id=1, source_target_pairs={{0,8},{8,16},{16,24},{24,32},{32,40},{40,48},{48,56},{56,64},{64,7... | collective-permute-start | bytes 86024 | tf_op jit(solution)/shard_map/ppermute | solution.py:19
  5.5 231.1 %collective-permute-start.1 = (f32[7,1024]{1,0:T(8,128)}, f32[7,1024]{1,0:T(8,128)}, u32[]{:S(2)}, u32[]{:S(2)}) collective-permute-start(f32[7,1024]{1,0:T(8,128)} %get-tuple-element.122), channel_id=1, source_target_pairs={{8,0},{16,8},{24,16},{32,24},{40,32},{48,40},{56,48},{64,56},{72,6... | collective-permute-start | bytes 86024 | tf_op jit(solution)/shard_map/ppermute | solution.py:21
  7.5 36.0 %copy-start.10 = (f32[8,3,64]{2,1,0:T(4,128)}, f32[8,3,64]{2,1,0:T(4,128)S(1)}, u32[]{:S(2)}) copy-start(f32[8,3,64]{2,1,0:T(4,128)S(1)} %copy.35) | copy-start | bytes 18436
  30.7 198.1 %collective-permute-start.3 = (f32[4,7,64]{2,1,0:T(8,128)}, f32[4,7,64]{2,1,0:T(8,128)}, u32[]{:S(2)}, u32[]{:S(2)}) collective-permute-start(f32[4,7,64]{2,1,0:T(8,128)} %get-tuple-element.149), channel_id=1, source_target_pairs={{8,0},{16,8},{24,16},{32,24},{40,32},{48,40},{56,48},{64,56},{72,6... | collective-permute-start | bytes 21512 | tf_op jit(solution)/shard_map/ppermute | solution.py:21
  32.0 196.8 %collective-permute-start.2 = (f32[4,7,64]{2,1,0:T(8,128)}, f32[4,7,64]{2,1,0:T(8,128)}, u32[]{:S(2)}, u32[]{:S(2)}) collective-permute-start(f32[4,7,64]{2,1,0:T(8,128)} %get-tuple-element.150), channel_id=1, source_target_pairs={{0,8},{8,16},{16,24},{24,32},{32,40},{40,48},{48,56},{56,64},{64,7... | collective-permute-start | bytes 21512 | tf_op jit(solution)/shard_map/ppermute | solution.py:19
  37.7 5.8 %copy-start.1 = (f32[252,64,64]{0,2,1:T(8,128)S(1)}, f32[252,64,64]{0,2,1:T(8,128)}, u32[]{:S(2)}) copy-start(f32[252,64,64]{0,2,1:T(8,128)} %param.16) | copy-start | bytes 12386308
  156.6 6.6 %slice-start = ((f32[252,64,64]{0,2,1:T(8,128)}), f32[64,64,64]{0,2,1:T(8,128)S(1)}, s32[]{:S(2)}) async-start(f32[252,64,64]{0,2,1:T(8,128)} %param.16), calls=%async_computation | async-start | bytes 4194304 | tf_op jit(solution)/shard_map/slice | solution.py:99
  166.0 3.1 %slice-start.1 = ((f32[252,64,64]{0,2,1:T(8,128)}), f32[128,64,64]{0,2,1:T(8,128)S(1)}, s32[]{:S(2)}) async-start(f32[252,64,64]{0,2,1:T(8,128)} %param.16), calls=%async_computation.1 | async-start | bytes 4194304 | tf_op jit(solution)/shard_map/slice | solution.py:99
  173.5 8.7 %copy-start.4 = (f32[64,64,64]{2,1,0:T(8,128)S(1)}, f32[64,64,64]{2,1,0:T(8,128)}, u32[]{:S(2)}) copy-start(f32[64,64,64]{2,1,0:T(8,128)} %copy.51) | copy-start | bytes 3145732
  182.2 3.5 %copy-start.5 = (f32[32,64,64]{2,1,0:T(8,128)S(1)}, f32[32,64,64]{2,1,0:T(8,128)}, u32[]{:S(2)}) copy-start(f32[32,64,64]{2,1,0:T(8,128)} %copy.53) | copy-start | bytes 1572868
  182.2 5.3 %copy-start.6 = (f32[16,64,64]{2,1,0:T(8,128)S(1)}, f32[16,64,64]{2,1,0:T(8,128)}, u32[]{:S(2)}) copy-start(f32[16,64,64]{2,1,0:T(8,128)} %copy.55) | copy-start | bytes 786436
  182.2 6.2 %copy-start.7 = (f32[8,64,64]{2,1,0:T(8,128)S(1)}, f32[8,64,64]{2,1,0:T(8,128)}, u32[]{:S(2)}) copy-start(f32[8,64,64]{2,1,0:T(8,128)} %copy.57) | copy-start | bytes 393220
  182.2 6.8 %copy-start.3 = (f32[4,64,64]{0,2,1:T(8,128)S(1)}, f32[4,64,64]{0,2,1:T(8,128)}, u32[]{:S(2)}) copy-start(f32[4,64,64]{0,2,1:T(8,128)} %slice.588) | copy-start | bytes 196612
  214.2 5.0 %copy-start.2 = (f32[254,3,64]{0,2,1:T(8,128)S(1)}, f32[254,3,64]{0,2,1:T(8,128)}, u32[]{:S(2)}) copy-start(f32[254,3,64]{0,2,1:T(8,128)} %param.17) | copy-start | bytes 585220
  218.4 9.0 %copy-start.14 = (f32[1,64,64]{2,1,0:T(8,128)S(1)}, f32[1,64,64]{2,1,0:T(8,128)}, u32[]{:S(2)}) copy-start(f32[1,64,64]{2,1,0:T(8,128)} %copy.52) | copy-start | bytes 49156
  218.4 9.4 %copy-start.13 = (f32[1,64,64]{2,1,0:T(8,128)S(1)}, f32[1,64,64]{2,1,0:T(8,128)}, u32[]{:S(2)}) copy-start(f32[1,64,64]{2,1,0:T(8,128)} %copy.50) | copy-start | bytes 49156
  218.4 9.8 %copy-start.12 = (f32[1,64,64]{2,1,0:T(8,128)S(1)}, f32[1,64,64]{2,1,0:T(8,128)}, u32[]{:S(2)}) copy-start(f32[1,64,64]{2,1,0:T(8,128)} %copy.48) | copy-start | bytes 49156
  218.4 10.4 %copy-start.11 = (f32[8,3,64]{2,1,0:T(4,128)S(1)}, f32[8,3,64]{2,1,0:T(4,128)}, u32[]{:S(2)}) copy-start(f32[8,3,64]{2,1,0:T(4,128)} %copy-done.10) | copy-start | bytes 18436
  218.4 11.2 %copy-start.18 = (f32[8,64]{1,0:T(8,128)S(1)}, f32[8,64]{1,0:T(8,128)}, u32[]{:S(2)}) copy-start(f32[8,64]{1,0:T(8,128)} %get-tuple-element.151) | copy-start | bytes 6148
  218.4 11.2 %copy-start.19 = (f32[8,64]{1,0:T(8,128)S(1)}, f32[8,64]{1,0:T(8,128)}, u32[]{:S(2)}) copy-start(f32[8,64]{1,0:T(8,128)} %get-tuple-element.152) | copy-start | bytes 6148
  218.4 11.2 %copy-start.20 = (f32[8,64]{1,0:T(8,128)S(1)}, f32[8,64]{1,0:T(8,128)}, u32[]{:S(2)}) copy-start(f32[8,64]{1,0:T(8,128)} %get-tuple-element.153) | copy-start | bytes 6148
  232.6 4.0 %copy-start.8 = (f32[4,2048]{1,0:T(4,128)S(1)}, f32[4,2048]{1,0:T(4,128)}, u32[]{:S(2)}) copy-start(f32[4,2048]{1,0:T(4,128)} %param.11) | copy-start | bytes 98308
  232.6 4.0 %copy-start.9 = (f32[3,2048]{1,0:T(4,128)S(1)}, f32[3,2048]{1,0:T(4,128)}, u32[]{:S(2)}) copy-start(f32[3,2048]{1,0:T(4,128)} %param.10) | copy-start | bytes 73732
  (3 other events, 3.1 us)
where the time goes:
time: 288 us; the launch traced here: 287 us
  blocking collectives  128 us (44%)
  local copies, waits for them, and re-layouts  64.8 us (22%)
  matrix products  53.6 us (19%)
  loops' own time  20.8 us (7%)
  starting transfers between devices  12.4 us (4%)
  other arithmetic  6.37 us (2%)
    all_gather x1, blocking collectives, on_device(): everyone = lax.all_gather(root[None], 'clus', axis=0, tiled=True)  107 us
    unnamed x55, local copies, waits for them, and re-layouts  34.2 us
    all_gather x1, blocking collectives, on_device(): basis = lax.all_gather(leaf_basis, 'rhs', axis=1, tiled=True)  21.2 us
    another operation x1, loops' own time, near_leaves(): return lax.map(near_leaf, indices)  20.8 us
    dot_general x8, matrix products, near_leaf(): return jnp.dot(window_rhs, block.T, precision=HIGHEST)  20.8 us
    dot_general x6, matrix products, on_device(): jnp.einsum('nab,nbc->nac', top_transfer[offset:offset + count], upward[le...  15.5 us
    dynamic_slice x1, local copies, waits for them, and re-layouts, on_device(): lax.dynamic_index_in_dim(top_transfer, offset + node, 0, keepdims=False)  12 us
    ppermute x2, starting transfers between devices, with_halo(): lax.ppermute(tail, axis, [(i, (i + 1) % count) for i in range(ends)])  9.84 us
  transfers between devices with their start and end apart: 4, of which 0 were waited for; matrix products, arithmetic and copies ran while one was open for 33% of the time, Pallas kernels for 0%

commit v1 on v0

v1 whole, which is shorter than its diff:
```python
import functools
import math

import jax
import jax.numpy as jnp
from jax import lax
from jax.experimental import pallas as pl
from jax.experimental.pallas import tpu as pltpu
from jax.sharding import PartitionSpec as P

AMPLITUDE = 0.2
INV_SCALE = 1.0 / (2.0 * 0.15 * 0.15)
COORD = math.sqrt(INV_SCALE * math.log2(math.e))
LOG_AMP = math.log2(AMPLITUDE)

F32 = jnp.float32
BF16 = jnp.bfloat16
MESH = pl.DeviceIdType.MESH

NN = (((1,), (0,)), ((), ()))
NT = (((1,), (1,)), ((), ()))
TN = (((0,), (0,)), ((), ()))

Y = 8
Z = 16
R = 64
LEAF = 256
LV = 8
COLS = 4
REACH = 4
SLOTS = 9
EXT = LV + 2 * REACH
HALO = REACH * LEAF


def split(x):
    hi = x.astype(BF16)
    return hi, (x - hi.astype(F32)).astype(BF16)


def dot(a, b, dims):
    return lax.dot_general(a, b, dims, preferred_element_type=F32)


def mm(a, b, dims):
    ah, al = split(a)
    bh, bl = split(b)
    return dot(ah, bh, dims) + (dot(ah, bl, dims) + dot(al, bh, dims))


def mtn(a, b):
    ah, al = split(a)
    bh, bl = split(b)
    return dot(jnp.concatenate([ah, ah, al], 0), jnp.concatenate([bh, bl, bh], 0), TN)


def rows8(x):
    hi = x.astype(BF16).astype(F32)
    return jnp.concatenate([hi, x - hi], 0)


def fold8(x):
    return x[0:COLS] + x[COLS : 2 * COLS]


def columns(seg):
    return jnp.concatenate([seg, jnp.zeros((5, seg.shape[1]), F32)], 0).T


def gauss(cols, rows):
    d0 = cols[0] - rows[0]
    d1 = cols[1] - rows[1]
    d2 = cols[2] - rows[2]
    return jnp.exp2(LOG_AMP - (d0 * d0 + d1 * d1 + d2 * d2))


def body(
    points, rhs, basis_in, nodes_in, lt_in, mask_in, top_t, top_n,
    out,
    pts, cols_s, lhs8, rh, nodes, mom, basis, lt, mask, wn,
    t0, t1, t2, t3, t4, t5, tn, upy, upz, m0, mz, ltc, qc, wd, pre, far8,
    lsem, bs_s, bs_r, hs_s, hs_r, ms_s, ms_r, ys_s, ys_r, zs_s, zs_r,
):
    c = lax.axis_index("clus")
    r = lax.axis_index("rhs")
    z = c // Y
    y = lax.rem(c, Y)
    n_clus = Y * Z
    nxt = lax.rem(c + 1, n_clus)
    prv = lax.rem(c + n_clus - 1, n_clus)

    r_peers = [(c, lax.rem(r + k, 8)) for k in range(1, 8)]
    y_peers = [(z * Y + lax.rem(y + k, Y), r) for k in range(1, Y)]
    z_peers = [(lax.rem(z + k, Z) * Y + y, r) for k in range(1, Z)]
    everyone = r_peers + y_peers + z_peers + [(nxt, r), (prv, r)]
    barrier = pltpu.get_barrier_semaphore()
    for p in everyone:
        pl.semaphore_signal(barrier, inc=1, device_id=p, device_id_type=MESH)

    own = pl.ds(HALO, LV * LEAF)
    loads = [
        (basis_in, basis.at[r]),
        (rhs, rh.at[:, own]),
        (lt_in, lt),
        (points, pts.at[:, own]),
        (nodes_in, nodes.at[pl.ds(REACH, LV)]),
        (mask_in, mask),
        (top_t.at[pl.ds(Y * z, Y)], t0),
        (top_t.at[pl.ds(128 + 4 * z, 4)], t1),
        (top_t.at[pl.ds(192 + 2 * z, 2)], t2),
        (top_t.at[pl.ds(224, 16)], t3),
        (top_t.at[pl.ds(240, 8)], t4),
        (top_t.at[pl.ds(248, 4)], t5),
    ]
    for b in range(7):
        off = 256 - 2 * (128 >> b)
        loads.append((top_n.at[pl.ds(off + 2 * (c >> (b + 1)), 2)], tn.at[b]))
    local = []
    for i, (src, dst) in enumerate(loads):
        cp = pltpu.make_async_copy(src, dst, lsem.at[i])
        cp.start()
        local.append(cp)

    pl.semaphore_wait(barrier, len(everyone))

    def remote(src, dst, s, q, to):
        cp = pltpu.make_async_remote_copy(
            src_ref=src, dst_ref=dst, send_sem=s, recv_sem=q, device_id=to, device_id_type=MESH
        )
        cp.start()
        return cp

    sent_b = [remote(basis_in, basis.at[r], bs_s.at[i], bs_r.at[i], p) for i, p in enumerate(r_peers)]
    right = pl.ds(LV * LEAF - HALO, HALO)
    left = pl.ds(0, HALO)
    to_left = pl.ds(0, HALO)
    to_right = pl.ds(HALO + LV * LEAF, HALO)
    sent_h = [
        remote(points.at[:, right], pts.at[:, to_left], hs_s.at[0], hs_r.at[0], (nxt, r)),
        remote(points.at[:, left], pts.at[:, to_right], hs_s.at[1], hs_r.at[1], (prv, r)),
        remote(rhs.at[:, right], rh.at[:, to_left], hs_s.at[2], hs_r.at[2], (nxt, r)),
        remote(rhs.at[:, left], rh.at[:, to_right], hs_s.at[3], hs_r.at[3], (prv, r)),
        remote(nodes_in.at[pl.ds(LV - REACH, REACH)], nodes.at[pl.ds(0, REACH)], hs_s.at[4], hs_r.at[4], (nxt, r)),
        remote(nodes_in.at[pl.ds(0, REACH)], nodes.at[pl.ds(REACH + LV, REACH)], hs_s.at[5], hs_r.at[5], (prv, r)),
    ]

    for cp in local:
        cp.wait()
    ltc[...] = jnp.concatenate([lt[g] for g in range(LV)], 1)
    q1 = [mm(t1[k], jnp.concatenate([t0[2 * k], t0[2 * k + 1]], 1), NN) for k in range(4)]
    qc[...] = jnp.concatenate(
        [mm(t2[k], jnp.concatenate([q1[2 * k], q1[2 * k + 1]], 1), NN) for k in range(2)], 1
    )
    path = [t0[y], t1[y >> 1], t2[y >> 2], t3[z], t4[z >> 1], t5[z >> 2]]
    e = None
    g_b = []
    for b in range(7):
        mine = lax.rem(c >> b, 2)
        mn = tn[b, pl.ds(mine, 1)][0] * COORD
        sn = tn[b, pl.ds(1 - mine, 1)][0] * COORD
        sc = columns(jnp.concatenate([sn, sn], 1))[0:R]
        s_t = gauss([sc[:, k : k + 1] for k in range(3)], [mn[k : k + 1] for k in range(3)])
        if b == 0:
            g_b.append(s_t)
        else:
            e = path[0] if b == 1 else mm(path[b - 1], e, NN)
            g_b.append(mm(s_t, e, NN))
    zero = jnp.zeros((R, R), F32)
    m0[y] = zero
    m0[y ^ 1] = g_b[0]
    s1 = (y >> 1) ^ 1
    for k in range(2):
        m0[2 * s1 + k] = mtn(t0[2 * s1 + k], g_b[1])
    s2 = (y >> 2) ^ 1
    for k in range(2):
        half = mtn(t1[2 * s2 + k], g_b[2])
        for j in range(2):
            m0[4 * s2 + 2 * k + j] = mtn(t0[4 * s2 + 2 * k + j], half)
    mz[z] = zero
    mz[z ^ 1] = g_b[3]
    s4 = (z >> 1) ^ 1
    for k in range(2):
        mz[2 * s4 + k] = mtn(t3[2 * s4 + k], g_b[4])
    s5 = (z >> 2) ^ 1
    for k in range(2):
        half = mtn(t4[2 * s5 + k], g_b[5])
        for j in range(2):
            mz[4 * s5 + 2 * k + j] = mtn(t3[4 * s5 + 2 * k + j], half)
    s6 = (z >> 3) ^ 1
    for i in range(2):
        top = mtn(t5[2 * s6 + i], g_b[6])
        for k in range(2):
            half = mtn(t4[4 * s6 + 2 * i + k], top)
            for j in range(2):
                mz[8 * s6 + 4 * i + 2 * k + j] = mtn(t3[8 * s6 + 4 * i + 2 * k + j], half)

    for cp in sent_b:
        cp.wait_recv()
    parts = []
    for g in range(LV):
        bg = basis[:, g].reshape(R, LEAF)
        parts.append(mm(rh[:, HALO + g * LEAF : HALO + (g + 1) * LEAF], bg, NT))
    moments = jnp.concatenate(parts, 1)
    mom[:, REACH * R : (REACH + LV) * R] = moments
    upy[y] = mm(moments, ltc[...], NT)
    sent_y = [remote(upy.at[y], upy.at[y], ys_s.at[i], ys_r.at[i], p) for i, p in enumerate(y_peers)]
    sent_m = [
        remote(mom.at[:, pl.ds(LV * R, REACH * R)], mom.at[:, pl.ds(0, REACH * R)], ms_s.at[0], ms_r.at[0], (nxt, r)),
        remote(mom.at[:, pl.ds(REACH * R, REACH * R)], mom.at[:, pl.ds((REACH + LV) * R, REACH * R)], ms_s.at[1], ms_r.at[1], (prv, r)),
    ]
    for g in range(LV):
        wd[:, g * LEAF : (g + 1) * LEAF] = mm(lt[g], basis[:, g].reshape(R, LEAF), NN)

    for cp in sent_y:
        cp.wait_recv()
    flat_y = jnp.concatenate([upy[k] for k in range(Y)], 1)
    upz[z] = mm(flat_y, qc[...], NT)
    sent_z = [remote(upz.at[z], upz.at[z], zs_s.at[i], zs_r.at[i], p) for i, p in enumerate(z_peers)]

    pre[...] = mm(flat_y, m0[...].reshape(Y * R, R), NN)

    for cp in sent_h:
        cp.wait_recv()
    lane = lax.broadcasted_iota(jnp.int32, (LV, SLOTS), 1)
    row = lax.broadcasted_iota(jnp.int32, (LV, SLOTS), 0)
    place = c * LV + row + lane - REACH
    valid = jnp.where((place >= 0) & (place < n_clus * LV), 1.0, 0.0).astype(F32)
    w = jnp.where(lane == REACH, 1.0, mask[...].astype(F32))
    wn[...] = w * valid
    wf = (1.0 - w) * valid

    skew = []
    for g in range(LV):
        piece = [wf[g : g + 1]]
        if g > 0:
            piece.insert(0, jnp.zeros((1, g), F32))
        if g < LV - 1:
            piece.append(jnp.zeros((1, LV - 1 - g), F32))
        skew.append(jnp.concatenate(piece, 1))
    skewed = jnp.concatenate(skew, 0)
    spread = jnp.where(
        lax.broadcasted_iota(jnp.int32, (LV, LV * R), 1) // R == lax.broadcasted_iota(jnp.int32, (LV, LV * R), 0),
        1.0, 0.0,
    ).astype(F32)
    far_w = dot(skewed, spread, TN)

    for cp in sent_m:
        cp.wait_recv()
    m8 = rows8(mom[...]).astype(BF16)
    flat_n = jnp.concatenate([nodes[l] for l in range(EXT)], 1) * COORD
    mine_n = flat_n[:, REACH * R : (REACH + LV) * R]
    targets = [mine_n[k : k + 1] for k in range(3)]
    acc = jnp.zeros((2 * COLS, LV * R), F32)
    for q in range(EXT // 4):
        hs, ls = [], []
        for p in range(2):
            cc = columns(flat_n[:, (2 * q + p) * 128 : (2 * q + p + 1) * 128])
            for u in range(2):
                l = 4 * q + 2 * p + u
                part = cc[u * R : (u + 1) * R]
                block = gauss([part[:, k : k + 1] for k in range(3)], targets) * far_w[l : l + 1]
                h, lo = split(block)
                hs.append(h)
                ls.append(lo)
        a = m8[:, q * 256 : (q + 1) * 256]
        acc = acc + dot(a, jnp.concatenate(hs, 0), NN) + dot(a, jnp.concatenate(ls, 0), NN)
    local_far = fold8(acc)
    for g in range(LV):
        far8[:, g * LEAF : (g + 1) * LEAF] = mm(
            local_far[:, g * R : (g + 1) * R], basis[:, g].reshape(R, LEAF), NN
        )

    lhs8[...] = rows8(rh[...])

    def prepare(l, _):
        for h in range(2):
            at = pl.multiple_of(l * LEAF + h * 128, 128)
            cc = columns(pts[:, pl.ds(at, 128)] * COORD)
            for k in range(3):
                cols_s[l, k, h * 128 : (h + 1) * 128] = jnp.broadcast_to(cc[:, k : k + 1], (128, 128))
        return 0

    lax.fori_loop(0, EXT, prepare, 0)

    def near(g, _):
        at = pl.multiple_of(HALO + g * LEAF, LEAF)
        tg = pts[:, pl.ds(at, LEAF)] * COORD
        wrow = wn[pl.ds(g, 1), :]
        accs = [jnp.zeros((2 * COLS, 128), F32) for _ in range(2)]
        for s in range(SLOTS):
            l = g + s
            a = (lhs8[:, pl.ds(pl.multiple_of(l * LEAF, LEAF), LEAF)] * wrow[:, s : s + 1]).astype(BF16)
            for h in range(2):
                k_hi, k_lo = split(
                    gauss(
                        [cols_s[l, k] for k in range(3)],
                        [tg[k : k + 1, h * 128 : (h + 1) * 128] for k in range(3)],
                    )
                )
                accs[h] = accs[h] + dot(a, k_hi, NN) + dot(a, k_lo, NN)
        to = pl.multiple_of(g * LEAF, LEAF)
        far8[:, pl.ds(to, LEAF)] = far8[:, pl.ds(to, LEAF)] + fold8(jnp.concatenate(accs, 1))
        return 0

    lax.fori_loop(0, LV, near, 0)

    for cp in sent_z:
        cp.wait_recv()
    flat_z = jnp.concatenate([upz[k] for k in range(Z)], 1)
    down = mm(flat_z, mz[...].reshape(Z * R, R), NN) + pre[...]
    out[...] = mm(down, wd[...], NN) + far8[...]

    for cp in sent_b + sent_h + sent_m + sent_y + sent_z:
        cp.wait_send()


def on_device(points, rhs_cols, leaf_basis, leaf_nodes, leaf_transfer, near_mask, top_transfer, top_nodes):
    any_space = pl.BlockSpec(memory_space=pl.ANY)
    dma = pltpu.SemaphoreType.DMA
    v = lambda *s: pltpu.VMEM(s, F32)
    return pl.pallas_call(
        body,
        out_shape=jax.ShapeDtypeStruct(rhs_cols.shape, F32),
        in_specs=[any_space] * 8,
        out_specs=pl.BlockSpec(memory_space=pltpu.VMEM),
        scratch_shapes=[
            v(3, EXT * LEAF),
            v(EXT, 3, LEAF, 128),
            v(2 * COLS, EXT * LEAF),
            v(COLS, EXT * LEAF),
            v(EXT, 3, R),
            v(COLS, EXT * R),
            v(8, LV, 8, LEAF),
            v(LV, R, R),
            pltpu.VMEM((LV, SLOTS), jnp.int32),
            v(LV, SLOTS),
            v(8, R, R), v(4, R, R), v(2, R, R), v(16, R, R), v(8, R, R), v(4, R, R),
            v(7, 2, 3, R),
            v(Y, COLS, R),
            v(Z, COLS, R),
            v(Y, R, R), v(Z, R, R),
            v(R, LV * R), v(R, Y * R),
            v(R, LV * LEAF),
            v(COLS, R),
            v(COLS, LV * LEAF),
            dma((19,)),
            dma((7,)), dma((7,)), dma((6,)), dma((6,)), dma((2,)), dma((2,)),
            dma((Y - 1,)), dma((Y - 1,)), dma((Z - 1,)), dma((Z - 1,)),
        ],
        compiler_params=pltpu.CompilerParams(
            collective_id=0, has_side_effects=True, vmem_limit_bytes=48 * 1024 * 1024
        ),
        cost_estimate=pl.CostEstimate(flops=10**9, bytes_accessed=4 * 10**6, transcendentals=5 * 10**6),
    )(points, rhs_cols, leaf_basis, leaf_nodes, leaf_transfer, near_mask, top_transfer, top_nodes)


def solution(mesh):
    return jax.shard_map(
        on_device,
        mesh=mesh,
        in_specs=(
            P(None, "clus"),
            P("rhs", "clus"),
            P("clus", "rhs", None),
            P("clus", None, None),
            P("clus", None, None),
            P("clus", None),
            P(),
            P(),
        ),
        out_specs=P("rhs", "clus"),
        check_vma=False,
    )
```

time: 288 us -> 65.4 us (0.23)
  the two profiles are of different devices: /device:TPU:2 before, /device:TPU:1 now
where the time goes in v1:
time: 65.4 us; the launch traced here: 65.2 us
  Pallas kernels  54.5 us (83%)
  local copies, waits for them, and re-layouts  10.6 us (16%)
    pallas_call x1, Pallas kernels, on_device(): pl.pallas_call(body, out_shape=jax.ShapeDtypeStruct(rhs_cols.shape, F32),...  54.5 us
    unnamed x14, local copies, waits for them, and re-layouts  10.6 us

profile of v1, /device:TPU:1, one launch (start us, length us, event | category | flops | bytes accessed | tf_op | source)
XLA Modules:
  0.0 65.2 jit_solution(11227292812335507578)
XLA Ops:
  0.0 0.0 copy-start.4
  0.0 0.0 copy-start
  0.0 0.0 copy-start.1
  0.0 0.0 copy-start.3
  0.0 0.0 copy-start.2
  0.0 0.8 %copy.9.nodes_in = f32[8,3,64]{2,1,0:T(4,128)S(1)} copy(f32[8,3,64]{2,0,1:T(8,128)} %param.11) | data formatting | bytes 12288 | tf_op args[3]
  0.8 1.2 %copy.11.top_n = f32[254,3,64]{2,1,0:T(4,128)S(1)} copy(f32[254,3,64]{0,2,1:T(8,128)} %param.15) | data formatting | bytes 390144 | tf_op args[7]
  2.0 8.1 %copy.10.top_t = f32[252,64,64]{2,1,0:T(8,128)} copy(f32[252,64,64]{0,2,1:T(8,128)} %param.14) | data formatting | bytes 8257536 | tf_op args[6]
  10.0 0.0 copy-done.4
  10.0 0.0 copy-done
  10.0 0.0 copy-done.1
  10.0 0.0 copy-done.3
  10.1 0.0 copy-done.2
  10.1 54.5 %shard_map.82 = f32[4,2048]{1,0:T(4,128)S(1)} custom-call(f32[3,2048]{1,0:T(4,128)S(1)} %copy-done.2, f32[4,2048]{1,0:T(4,128)S(1)} %copy-done.3, f32[8,8,256]{2,1,0:T(8,128)S(1)} %copy-done.1, f32[8,3,64]{2,1,0:T(4,128)S(1)} %copy.9.nodes_in, f32[8,64,64]{2,1,0:T(8,128)S(1)} %copy-done, s32[8,9]{1,0:T(8,128)S(1)} %copy-done.4, f32[252,64,64]{2,1,0:T(8,128)} %copy.10.top_t, ...), custom_call_target="tpu_custom_call" | custom-call | flops 1000000000 | bytes 4000000 | tf_op jit(solution)/shard_map/pallas_call | solution.py:321
  64.5 0.6 copy.13
Async XLA Ops:
  0.0 10.0 %copy-start.4 = (s32[8,9]{1,0:T(8,128)S(1)}, s32[8,9]{1,0:T(8,128)}, u32[]{:S(2)}) copy-start(s32[8,9]{1,0:T(8,128)} %mask_in.1) | copy-start | bytes 868
  0.0 10.0 %copy-start = (f32[8,64,64]{2,1,0:T(8,128)S(1)}, f32[8,64,64]{2,1,0:T(8,128)}, u32[]{:S(2)}) copy-start(f32[8,64,64]{2,1,0:T(8,128)} %lt_in.1) | copy-start | bytes 393220
  0.0 10.0 %copy-start.1 = (f32[8,8,256]{2,1,0:T(8,128)S(1)}, f32[8,8,256]{2,1,0:T(8,128)}, u32[]{:S(2)}) copy-start(f32[8,8,256]{2,1,0:T(8,128)} %basis_in.1) | copy-start | bytes 196612
  0.0 10.0 %copy-start.3 = (f32[4,2048]{1,0:T(4,128)S(1)}, f32[4,2048]{1,0:T(4,128)}, u32[]{:S(2)}) copy-start(f32[4,2048]{1,0:T(4,128)} %rhs.1) | copy-start | bytes 98308
  0.0 10.0 %copy-start.2 = (f32[3,2048]{1,0:T(4,128)S(1)}, f32[3,2048]{1,0:T(4,128)}, u32[]{:S(2)}) copy-start(f32[3,2048]{1,0:T(4,128)} %points.1) | copy-start | bytes 73732

commit v2 on v1

v2 whole, which is shorter than its diff:
```python
import functools
import math

import jax
import jax.numpy as jnp
from jax import lax
from jax.experimental import pallas as pl
from jax.experimental.pallas import tpu as pltpu
from jax.sharding import PartitionSpec as P

AMPLITUDE = 0.2
INV_SCALE = 1.0 / (2.0 * 0.15 * 0.15)
COORD = math.sqrt(INV_SCALE * math.log2(math.e))
LOG_AMP = math.log2(AMPLITUDE)

F32 = jnp.float32
BF16 = jnp.bfloat16
MESH = pl.DeviceIdType.MESH

NN = (((1,), (0,)), ((), ()))
NT = (((1,), (1,)), ((), ()))
TN = (((0,), (0,)), ((), ()))

Y = 8
Z = 16
R = 64
LEAF = 256
LV = 8
COLS = 4
REACH = 4
SLOTS = 9
EXT = LV + 2 * REACH
HALO = REACH * LEAF


def split(x):
    hi = x.astype(BF16)
    return hi, (x - hi.astype(F32)).astype(BF16)


def dot(a, b, dims):
    return lax.dot_general(a, b, dims, preferred_element_type=F32)


def mm(a, b, dims):
    ah, al = split(a)
    bh, bl = split(b)
    return dot(ah, bh, dims) + (dot(ah, bl, dims) + dot(al, bh, dims))


def mtn(a, b):
    ah, al = split(a)
    bh, bl = split(b)
    return dot(jnp.concatenate([ah, ah, al], 0), jnp.concatenate([bh, bl, bh], 0), TN)


def rows8(x):
    hi = x.astype(BF16).astype(F32)
    return jnp.concatenate([hi, x - hi], 0)


def fold8(x):
    return x[0:COLS] + x[COLS : 2 * COLS]


def columns(seg):
    return jnp.concatenate([seg, jnp.zeros((5, seg.shape[1]), F32)], 0).T


def gauss(cols, rows):
    d0 = cols[0] - rows[0]
    d1 = cols[1] - rows[1]
    d2 = cols[2] - rows[2]
    return jnp.exp2(LOG_AMP - (d0 * d0 + d1 * d1 + d2 * d2))


class Refs:
    pass


def extract(t):
    def turn(a, _):
        slab = t.slab[a]
        low = slab[:, 0:128].T
        high = jnp.concatenate([slab[:, 128:], jnp.zeros((R, 256 - t.n_top), F32)], 1).T
        t.turned[pl.ds(pl.multiple_of(a * 256, 256), 128), :] = low
        t.turned[pl.ds(pl.multiple_of(a * 256 + 128, 128), 128), :] = high
        return 0

    lax.fori_loop(0, R, turn, 0, unroll=4)
    for k in range(3):
        x = t.nslab[k] * COORD
        t.nturned[k, 0:128] = x[:, 0:128].T
        t.nturned[k, 128:256] = jnp.concatenate([x[:, 128:], jnp.zeros((R, 2), F32)], 1).T


def operators(t):
    z, y, c = t.z, t.y, t.c

    def top(n):
        return t.turned[pl.ds(n, R, stride=256), :]

    t0 = lambda k: top(Y * z + k)
    t1 = lambda k: top(128 + 4 * z + k)
    t2 = lambda k: top(192 + 2 * z + k)
    t3 = lambda k: top(224 + k)
    t4 = lambda k: top(240 + k)
    t5 = lambda k: top(248 + k)
    q1 = [mm(t1(k), jnp.concatenate([t0(2 * k), t0(2 * k + 1)], 1), NN) for k in range(4)]
    t.qc[...] = jnp.concatenate(
        [mm(t2(k), jnp.concatenate([q1[2 * k], q1[2 * k + 1]], 1), NN) for k in range(2)], 1
    )
    path = [t0(y), t1(y >> 1), t2(y >> 2), t3(z), t4(z >> 1), t5(z >> 2)]
    e = None
    g_b = []
    for b in range(7):
        off = 256 - 2 * (128 >> b)
        at = off + (c >> b)
        sib = off + ((c >> b) ^ 1)
        mn = [t.nturned[k, pl.ds(at, 1)] for k in range(3)]
        sn = jnp.concatenate([t.nturned[k, pl.ds(sib, 1)] for k in range(3)], 0)
        sc = columns(jnp.concatenate([sn, sn], 1))[0:R]
        s_t = gauss([sc[:, k : k + 1] for k in range(3)], mn)
        if b == 0:
            g_b.append(s_t)
        else:
            e = path[0] if b == 1 else mm(path[b - 1], e, NN)
            g_b.append(mm(s_t, e, NN))
    zero = jnp.zeros((R, R), F32)
    m0, mz = t.m0, t.mz
    m0[y] = zero
    m0[y ^ 1] = g_b[0]
    s1 = (y >> 1) ^ 1
    for k in range(2):
        m0[2 * s1 + k] = mtn(t0(2 * s1 + k), g_b[1])
    s2 = (y >> 2) ^ 1
    for k in range(2):
        half = mtn(t1(2 * s2 + k), g_b[2])
        for j in range(2):
            m0[4 * s2 + 2 * k + j] = mtn(t0(4 * s2 + 2 * k + j), half)
    mz[z] = zero
    mz[z ^ 1] = g_b[3]
    s4 = (z >> 1) ^ 1
    for k in range(2):
        mz[2 * s4 + k] = mtn(t3(2 * s4 + k), g_b[4])
    s5 = (z >> 2) ^ 1
    for k in range(2):
        half = mtn(t4(2 * s5 + k), g_b[5])
        for j in range(2):
            mz[4 * s5 + 2 * k + j] = mtn(t3(4 * s5 + 2 * k + j), half)
    s6 = (z >> 3) ^ 1
    for i in range(2):
        up = mtn(t5(2 * s6 + i), g_b[6])
        for k in range(2):
            half = mtn(t4(4 * s6 + 2 * i + k), up)
            for j in range(2):
                mz[8 * s6 + 4 * i + 2 * k + j] = mtn(t3(8 * s6 + 4 * i + 2 * k + j), half)


def leaf_basis_of(t, g):
    return t.basis[:, g].reshape(R, LEAF)


def gather_transfers(t):
    t.ltc[...] = jnp.concatenate([t.lt[g] for g in range(LV)], 1)


def expand(t):
    parts = []
    for g in range(LV):
        parts.append(mm(t.rh[:, HALO + g * LEAF : HALO + (g + 1) * LEAF], leaf_basis_of(t, g), NT))
    moments = jnp.concatenate(parts, 1)
    t.mom[:, REACH * R : (REACH + LV) * R] = moments
    t.upy[t.y] = mm(moments, t.ltc[...], NT)


def lift_basis(t):
    for g in range(LV):
        t.wd[:, g * LEAF : (g + 1) * LEAF] = mm(t.lt[g], leaf_basis_of(t, g), NN)


def weights(t):
    lane = lax.broadcasted_iota(jnp.int32, (LV, SLOTS), 1)
    row = lax.broadcasted_iota(jnp.int32, (LV, SLOTS), 0)
    place = t.c * LV + row + lane - REACH
    valid = jnp.where((place >= 0) & (place < Y * Z * LV), 1.0, 0.0).astype(F32)
    w = jnp.where(lane == REACH, 1.0, t.mask[...].astype(F32))
    t.wn[...] = w * valid
    wf = (1.0 - w) * valid
    skew = []
    for g in range(LV):
        piece = [wf[g : g + 1]]
        if g > 0:
            piece.insert(0, jnp.zeros((1, g), F32))
        if g < LV - 1:
            piece.append(jnp.zeros((1, LV - 1 - g), F32))
        skew.append(jnp.concatenate(piece, 1))
    skewed = jnp.concatenate(skew, 0)
    spread = jnp.where(
        lax.broadcasted_iota(jnp.int32, (LV, LV * R), 1) // R == lax.broadcasted_iota(jnp.int32, (LV, LV * R), 0),
        1.0, 0.0,
    ).astype(F32)
    t.fw[...] = dot(skewed, spread, TN)


def leaf_far(t):
    m8 = rows8(t.mom[...]).astype(BF16)
    flat = []
    for k in range(3):
        rows = [t.nodes[0, k, l : l + 1] for l in range(LV - REACH, LV)]
        rows += [t.nodes[1, k, l : l + 1] for l in range(LV)]
        rows += [t.nodes[2, k, l : l + 1] for l in range(REACH)]
        flat.append(jnp.concatenate(rows, 1))
    flat_n = jnp.concatenate(flat, 0) * COORD
    mine_n = flat_n[:, REACH * R : (REACH + LV) * R]
    targets = [mine_n[k : k + 1] for k in range(3)]
    far_w = t.fw[...]
    acc = jnp.zeros((2 * COLS, LV * R), F32)
    for q in range(EXT // 4):
        hs, ls = [], []
        for p in range(2):
            cc = columns(flat_n[:, (2 * q + p) * 128 : (2 * q + p + 1) * 128])
            for u in range(2):
                l = 4 * q + 2 * p + u
                part = cc[u * R : (u + 1) * R]
                block = gauss([part[:, k : k + 1] for k in range(3)], targets) * far_w[l : l + 1]
                h, lo = split(block)
                hs.append(h)
                ls.append(lo)
        a = m8[:, q * 256 : (q + 1) * 256]
        acc = acc + dot(a, jnp.concatenate(hs, 0), NN) + dot(a, jnp.concatenate(ls, 0), NN)
    local_far = fold8(acc)
    for g in range(LV):
        cut = slice(g * LEAF, (g + 1) * LEAF)
        t.far8[:, cut] = t.far8[:, cut] + mm(local_far[:, g * R : (g + 1) * R], leaf_basis_of(t, g), NN)


def source_columns(t, first, count):
    def prepare(l, _):
        for h in range(2):
            at = pl.multiple_of(l * LEAF + h * 128, 128)
            cc = columns(t.pts[:, pl.ds(at, 128)] * COORD)
            for k in range(3):
                t.cols_s[l, k, h * 128 : (h + 1) * 128] = jnp.broadcast_to(cc[:, k : k + 1], (128, 128))
        at = pl.multiple_of(l * LEAF, LEAF)
        t.lhs8[:, pl.ds(at, LEAF)] = rows8(t.rh[:, pl.ds(at, LEAF)])
        return 0

    lax.fori_loop(first, first + count, prepare, 0)


def near(t, first, count):
    def leaf(g, _):
        at = pl.multiple_of(HALO + g * LEAF, LEAF)
        tg = t.pts[:, pl.ds(at, LEAF)] * COORD
        wrow = t.wn[pl.ds(g, 1), :]
        accs = [jnp.zeros((2 * COLS, 128), F32) for _ in range(2)]
        for s in range(SLOTS):
            l = g + s
            a = (t.lhs8[:, pl.ds(pl.multiple_of(l * LEAF, LEAF), LEAF)] * wrow[:, s : s + 1]).astype(BF16)
            for h in range(2):
                k_hi, k_lo = split(
                    gauss(
                        [t.cols_s[l, k] for k in range(3)],
                        [tg[k : k + 1, h * 128 : (h + 1) * 128] for k in range(3)],
                    )
                )
                accs[h] = accs[h] + dot(a, k_hi, NN) + dot(a, k_lo, NN)
        to = pl.multiple_of(g * LEAF, LEAF)
        t.far8[:, pl.ds(to, LEAF)] = fold8(jnp.concatenate(accs, 1))
        return 0

    lax.fori_loop(first, first + count, leaf, 0)


def level_three(t):
    flat_y = jnp.concatenate([t.upy[k] for k in range(Y)], 1)
    t.upz[t.z] = mm(flat_y, t.qc[...], NT)


def lower_levels(t):
    flat_y = jnp.concatenate([t.upy[k] for k in range(Y)], 1)
    t.pre[...] = mm(flat_y, t.m0[...].reshape(Y * R, R), NN)


def finish(t):
    flat_z = jnp.concatenate([t.upz[k] for k in range(Z)], 1)
    down = mm(flat_z, t.mz[...].reshape(Z * R, R), NN) + t.pre[...]
    t.out[...] = mm(down, t.wd[...], NN) + t.far8[...]


def vm(*s):
    return pltpu.VMEM(s, F32)


SCRATCH = dict(
    pts=vm(3, EXT * LEAF),
    cols_s=vm(EXT, 3, LEAF, 128),
    lhs8=vm(2 * COLS, EXT * LEAF),
    rh=vm(COLS, EXT * LEAF),
    nodes=vm(3, 3, LV, R),
    mom=vm(COLS, EXT * R),
    basis=vm(8, LV, 8, LEAF),
    lt=vm(LV, R, R),
    mask=pltpu.VMEM((LV, SLOTS), jnp.int32),
    wn=vm(LV, SLOTS),
    fw=vm(EXT, LV * R),
    slab=vm(R, R, 252),
    turned=vm(R * 256, R),
    nslab=vm(3, R, 254),
    nturned=vm(3, 256, R),
    upy=vm(Y, COLS, R),
    upz=vm(Z, COLS, R),
    m0=vm(Y, R, R),
    mz=vm(Z, R, R),
    ltc=vm(R, LV * R),
    qc=vm(R, Y * R),
    wd=vm(R, LV * LEAF),
    pre=vm(COLS, R),
    far8=vm(COLS, LV * LEAF),
)

DMA = pltpu.SemaphoreType.DMA
SEMS = dict(
    lsem=DMA((8,)),
    bs=DMA((2, 7)),
    hs=DMA((2, 6)),
    ms=DMA((2, 2)),
    ys=DMA((2, Y - 1)),
    zs=DMA((2, Z - 1)),
)


def body(points, rhs, basis_in, nodes_in, lt_in, mask_in, top_t, top_n, out, *rest):
    t = Refs()
    for name, ref in zip([*SCRATCH, *SEMS], rest):
        setattr(t, name, ref)
    t.out = out
    t.n_top = top_t.shape[2]
    c = lax.axis_index("clus")
    r = lax.axis_index("rhs")
    z = c // Y
    y = lax.rem(c, Y)
    t.c, t.z, t.y = c, z, y
    n_clus = Y * Z
    nxt = lax.rem(c + 1, n_clus)
    prv = lax.rem(c + n_clus - 1, n_clus)

    r_peers = [(c, lax.rem(r + k, 8)) for k in range(1, 8)]
    y_peers = [(z * Y + lax.rem(y + k, Y), r) for k in range(1, Y)]
    z_peers = [(lax.rem(z + k, Z) * Y + y, r) for k in range(1, Z)]
    everyone = r_peers + y_peers + z_peers + [(nxt, r), (prv, r)]
    barrier = pltpu.get_barrier_semaphore()
    for p in everyone:
        pl.semaphore_signal(barrier, inc=1, device_id=p, device_id_type=MESH)

    own = pl.ds(HALO, LV * LEAF)
    loads = [
        (top_n, t.nslab),
        (top_t, t.slab),
        (points, t.pts.at[:, own]),
        (rhs, t.rh.at[:, own]),
        (mask_in, t.mask),
        (lt_in, t.lt),
        (nodes_in, t.nodes.at[1]),
        (basis_in, t.basis.at[r]),
    ]
    local = []
    for i, (src, dst) in enumerate(loads):
        cp = pltpu.make_async_copy(src, dst, t.lsem.at[i])
        cp.start()
        local.append(cp)

    def remote(src, dst, sem, i, to):
        cp = pltpu.make_async_remote_copy(
            src_ref=src, dst_ref=dst, send_sem=sem.at[0, i], recv_sem=sem.at[1, i], device_id=to, device_id_type=MESH
        )
        cp.start()
        return cp

    pl.semaphore_wait(barrier, len(everyone))

    sent_b = [remote(basis_in, t.basis.at[r], t.bs, i, p) for i, p in enumerate(r_peers)]
    right = pl.ds(LV * LEAF - HALO, HALO)
    left = pl.ds(0, HALO)
    to_left = pl.ds(0, HALO)
    to_right = pl.ds(HALO + LV * LEAF, HALO)
    sent_h = [
        remote(points.at[:, right], t.pts.at[:, to_left], t.hs, 0, (nxt, r)),
        remote(points.at[:, left], t.pts.at[:, to_right], t.hs, 1, (prv, r)),
        remote(rhs.at[:, right], t.rh.at[:, to_left], t.hs, 2, (nxt, r)),
        remote(rhs.at[:, left], t.rh.at[:, to_right], t.hs, 3, (prv, r)),
        remote(nodes_in, t.nodes.at[0], t.hs, 4, (nxt, r)),
        remote(nodes_in, t.nodes.at[2], t.hs, 5, (prv, r)),
    ]
    for cp in local:
        cp.wait()
    extract(t)
    operators(t)
    gather_transfers(t)
    weights(t)

    for cp in sent_b:
        cp.wait_recv()
    expand(t)
    sent_y = [remote(t.upy.at[y], t.upy.at[y], t.ys, i, p) for i, p in enumerate(y_peers)]
    out_r = pl.ds(LV * R, REACH * R)
    out_l = pl.ds(REACH * R, REACH * R)
    sent_m = [
        remote(t.mom.at[:, out_r], t.mom.at[:, pl.ds(0, REACH * R)], t.ms, 0, (nxt, r)),
        remote(t.mom.at[:, out_l], t.mom.at[:, pl.ds((REACH + LV) * R, REACH * R)], t.ms, 1, (prv, r)),
    ]
    lift_basis(t)
    ahead = jnp.where(z < Z // 2, LV, 0)
    for cp in sent_h:
        cp.wait_recv()
    source_columns(t, 0, EXT)
    near(t, 0, ahead)

    for cp in sent_y:
        cp.wait_recv()
    level_three(t)
    sent_z = [remote(t.upz.at[z], t.upz.at[z], t.zs, i, p) for i, p in enumerate(z_peers)]
    lower_levels(t)
    near(t, ahead, LV - ahead)
    for cp in sent_m:
        cp.wait_recv()
    leaf_far(t)

    for cp in sent_z:
        cp.wait_recv()
    finish(t)
    for cp in sent_b + sent_h + sent_m + sent_y + sent_z:
        cp.wait_send()


def on_device(points, rhs_cols, leaf_basis, leaf_nodes, leaf_transfer, near_mask, top_transfer, top_nodes):
    hbm = pl.BlockSpec(memory_space=pltpu.HBM)
    return pl.pallas_call(
        body,
        out_shape=jax.ShapeDtypeStruct(rhs_cols.shape, F32),
        in_specs=[hbm] * 8,
        out_specs=pl.BlockSpec(memory_space=pltpu.VMEM),
        scratch_shapes=[*SCRATCH.values(), *SEMS.values()],
        compiler_params=pltpu.CompilerParams(
            collective_id=0, has_side_effects=True, vmem_limit_bytes=58 * 1024 * 1024
        ),
        cost_estimate=pl.CostEstimate(flops=10**9, bytes_accessed=4 * 10**6, transcendentals=5 * 10**6),
    )(
        points, rhs_cols, leaf_basis, jnp.transpose(leaf_nodes, (1, 0, 2)), leaf_transfer, near_mask,
        jnp.transpose(top_transfer, (1, 2, 0)), jnp.transpose(top_nodes, (1, 2, 0)),
    )


def solution(mesh):
    return jax.shard_map(
        on_device,
        mesh=mesh,
        in_specs=(
            P(None, "clus"),
            P("rhs", "clus"),
            P("clus", "rhs", None),
            P("clus", None, None),
            P("clus", None, None),
            P("clus", None),
            P(),
            P(),
        ),
        out_specs=P("rhs", "clus"),
        check_vma=False,
    )
```

time: 65.4 us -> 55.9 us (0.85)
  local copies, waits for them, and re-layouts: 10.6 us -> 1.38 us
    unnamed x14 -> x1, local copies, waits for them, and re-layouts: 10.6 us -> 1.38 us
where the time goes in v2:
time: 55.9 us; the launch traced here: 55.7 us
  Pallas kernels  54.3 us (97%)
  local copies, waits for them, and re-layouts  1.38 us (2%)
    pallas_call x1, Pallas kernels, on_device(): pl.pallas_call(body, out_shape=jax.ShapeDtypeStruct(rhs_cols.shape, F32),...  54.3 us
    unnamed x1, local copies, waits for them, and re-layouts  1.38 us

profile of v2, /device:TPU:1, one launch (start us, length us, event | category | flops | bytes accessed | tf_op | source)
XLA Modules:
  0.0 55.7 jit_solution(1863510490884024604)
XLA Ops:
  0.0 54.3 %shard_map.82 = f32[4,2048]{1,0:T(4,128)} custom-call(f32[3,2048]{1,0:T(4,128)} %points.1, f32[4,2048]{1,0:T(4,128)} %rhs.1, f32[8,8,256]{2,1,0:T(8,128)} %basis_in.1, f32[3,8,64]{2,1,0:T(8,128)} %bitcast.5, f32[8,64,64]{2,1,0:T(8,128)} %lt_in.1, s32[8,9]{1,0:T(8,128)} %mask_in.1, f32[64,64,252]{2,1,0:T(8,128)} %bitcast.3, f32[3,64,254]{2,1,0:T(8,128)} %bitcast.4), custom_call_target="tpu_custom_call" | custom-call | flops 1000000000 | bytes 4000000 | tf_op jit(solution)/shard_map/pallas_call | solution.py:439
  54.3 1.4 %copy.10 = f32[4,2048]{1,0:T(4,128)} copy(f32[4,2048]{1,0:T(4,128)} %shard_map.82) | data formatting | bytes 65536

commit v3 on v2

--- a/solution.py
+++ b/solution.py
@@ -31,6 +31,7 @@
 SLOTS = 9
 EXT = LV + 2 * REACH
 HALO = REACH * LEAF
+AHEAD = 3
 
 
 def split(x):
@@ -235,14 +236,26 @@
         t.far8[:, cut] = t.far8[:, cut] + mm(local_far[:, g * R : (g + 1) * R], leaf_basis_of(t, g), NN)
 
 
-def source_columns(t, first, count):
+def three(x):
+    h = x.astype(BF16).astype(F32)
+    m = (x - h).astype(BF16).astype(F32)
+    return h, m, (x - h - m).astype(BF16).astype(F32)
+
+
+def sources(t, first, count):
     def prepare(l, _):
-        for h in range(2):
-            at = pl.multiple_of(l * LEAF + h * 128, 128)
-            cc = columns(t.pts[:, pl.ds(at, 128)] * COORD)
-            for k in range(3):
-                t.cols_s[l, k, h * 128 : (h + 1) * 128] = jnp.broadcast_to(cc[:, k : k + 1], (128, 128))
         at = pl.multiple_of(l * LEAF, LEAF)
+        x = (t.pts[:, pl.ds(at, LEAF)] - 0.5) * COORD
+        h, m, lo = three(x)
+        sq = x * x
+        n = sq[0:1] + sq[1:2] + sq[2:3]
+        one = jnp.ones((3, LEAF), F32)
+        rows = jnp.concatenate([h, h, m, h, lo, m, *[-v for v in three(n)], one, jnp.zeros((8, LEAF), F32)], 0)
+        for u in range(2):
+            t.a_s[pl.ds(pl.multiple_of(at + u * 128, 128), 128), :] = rows[:, u * 128 : (u + 1) * 128].T.astype(BF16)
+        t.b_s[:, pl.ds(at, LEAF)] = jnp.concatenate(
+            [h, m, h, lo, h, m, 0.5 * one, *[0.5 * v for v in three(LOG_AMP - n)], jnp.zeros((8, LEAF), F32)], 0
+        ).astype(BF16) * 2
         t.lhs8[:, pl.ds(at, LEAF)] = rows8(t.rh[:, pl.ds(at, LEAF)])
         return 0
 
@@ -251,23 +264,16 @@
 
 def near(t, first, count):
     def leaf(g, _):
-        at = pl.multiple_of(HALO + g * LEAF, LEAF)
-        tg = t.pts[:, pl.ds(at, LEAF)] * COORD
+        b = t.b_s[:, pl.ds(pl.multiple_of(HALO + g * LEAF, LEAF), LEAF)]
         wrow = t.wn[pl.ds(g, 1), :]
-        accs = [jnp.zeros((2 * COLS, 128), F32) for _ in range(2)]
+        acc = jnp.zeros((2 * COLS, LEAF), F32)
         for s in range(SLOTS):
-            l = g + s
-            a = (t.lhs8[:, pl.ds(pl.multiple_of(l * LEAF, LEAF), LEAF)] * wrow[:, s : s + 1]).astype(BF16)
-            for h in range(2):
-                k_hi, k_lo = split(
-                    gauss(
-                        [t.cols_s[l, k] for k in range(3)],
-                        [tg[k : k + 1, h * 128 : (h + 1) * 128] for k in range(3)],
-                    )
-                )
-                accs[h] = accs[h] + dot(a, k_hi, NN) + dot(a, k_lo, NN)
+            at = pl.multiple_of((g + s) * LEAF, LEAF)
+            a = (t.lhs8[:, pl.ds(at, LEAF)] * wrow[:, s : s + 1]).astype(BF16)
+            k_hi, k_lo = split(jnp.exp2(dot(t.a_s[pl.ds(at, LEAF), :], b, NN)))
+            acc = acc + dot(a, k_hi, NN) + dot(a, k_lo, NN)
         to = pl.multiple_of(g * LEAF, LEAF)
-        t.far8[:, pl.ds(to, LEAF)] = fold8(jnp.concatenate(accs, 1))
+        t.far8[:, pl.ds(to, LEAF)] = fold8(acc)
         return 0
 
     lax.fori_loop(first, first + count, leaf, 0)
@@ -295,7 +301,8 @@
 
 SCRATCH = dict(
     pts=vm(3, EXT * LEAF),
-    cols_s=vm(EXT, 3, LEAF, 128),
+    a_s=pltpu.VMEM((EXT * LEAF, 32), BF16),
+    b_s=pltpu.VMEM((32, EXT * LEAF), BF16),
     lhs8=vm(2 * COLS, EXT * LEAF),
     rh=vm(COLS, EXT * LEAF),
     nodes=vm(3, 3, LV, R),
@@ -328,6 +335,7 @@
     ms=DMA((2, 2)),
     ys=DMA((2, Y - 1)),
     zs=DMA((2, Z - 1)),
+    known=pltpu.SemaphoreType.REGULAR((3,)),
 )
 
 
@@ -347,12 +355,18 @@
     prv = lax.rem(c + n_clus - 1, n_clus)
 
     r_peers = [(c, lax.rem(r + k, 8)) for k in range(1, 8)]
-    y_peers = [(z * Y + lax.rem(y + k, Y), r) for k in range(1, Y)]
-    z_peers = [(lax.rem(z + k, Z) * Y + y, r) for k in range(1, Z)]
-    everyone = r_peers + y_peers + z_peers + [(nxt, r), (prv, r)]
+    y_at = lambda k: (z * Y + lax.rem(y + Y + k, Y), r)
+    z_at = lambda k: (lax.rem(z + Z + k, Z) * Y + y, r)
+    y_peers = [y_at(k) for k in range(1, Y)]
+    z_peers = [z_at(k) for k in range(1, Z)]
+
+    def signal(sem, p):
+        pl.semaphore_signal(sem, inc=1, device_id=p, device_id_type=MESH)
+
+    neighbours = r_peers + [y_at(1), y_at(-1), z_at(1), z_at(-1), (nxt, r), (prv, r)]
     barrier = pltpu.get_barrier_semaphore()
-    for p in everyone:
-        pl.semaphore_signal(barrier, inc=1, device_id=p, device_id_type=MESH)
+    for p in neighbours:
+        signal(barrier, p)
 
     own = pl.ds(HALO, LV * LEAF)
     loads = [
@@ -378,7 +392,7 @@
         cp.start()
         return cp
 
-    pl.semaphore_wait(barrier, len(everyone))
+    pl.semaphore_wait(barrier, len(neighbours))
 
     sent_b = [remote(basis_in, t.basis.at[r], t.bs, i, p) for i, p in enumerate(r_peers)]
     right = pl.ds(LV * LEAF - HALO, HALO)
@@ -393,10 +407,18 @@
         remote(nodes_in, t.nodes.at[0], t.hs, 4, (nxt, r)),
         remote(nodes_in, t.nodes.at[2], t.hs, 5, (prv, r)),
     ]
+    for p in (y_at(1), y_at(-1), z_at(1), z_at(-1)):
+        signal(t.known.at[0], p)
     for cp in local:
         cp.wait()
     extract(t)
+    pl.semaphore_wait(t.known.at[0], 4)
+    for p in (y_at(2), y_at(-2), z_at(2), z_at(-2)):
+        signal(t.known.at[1], p)
     operators(t)
+    pl.semaphore_wait(t.known.at[1], 4)
+    for p in (z_at(4), z_at(-4)):
+        signal(t.known.at[2], p)
     gather_transfers(t)
     weights(t)
 
@@ -411,18 +433,18 @@
         remote(t.mom.at[:, out_l], t.mom.at[:, pl.ds((REACH + LV) * R, REACH * R)], t.ms, 1, (prv, r)),
     ]
     lift_basis(t)
-    ahead = jnp.where(z < Z // 2, LV, 0)
     for cp in sent_h:
         cp.wait_recv()
-    source_columns(t, 0, EXT)
-    near(t, 0, ahead)
-
+    sources(t, 0, EXT)
+    near(t, 0, AHEAD)
+
+    pl.semaphore_wait(t.known.at[2], 2)
     for cp in sent_y:
         cp.wait_recv()
     level_three(t)
     sent_z = [remote(t.upz.at[z], t.upz.at[z], t.zs, i, p) for i, p in enumerate(z_peers)]
     lower_levels(t)
-    near(t, ahead, LV - ahead)
+    near(t, AHEAD, LV - AHEAD)
     for cp in sent_m:
         cp.wait_recv()
     leaf_far(t)

time: 55.9 us -> 46.7 us (0.84)
  Pallas kernels: 54.3 us -> 45.1 us
    pallas_call x1, Pallas kernels: 54.3 us -> 45.1 us  [on_device(): pl.pallas_call(body, out_shape=jax.ShapeDtypeStruct(rhs_cols.shape, F32),...]
where the time goes in v3:
time: 46.7 us; the launch traced here: 46.5 us
  Pallas kernels  45.1 us (97%)
  local copies, waits for them, and re-layouts  1.38 us (3%)
    pallas_call x1, Pallas kernels, on_device(): pl.pallas_call(body, out_shape=jax.ShapeDtypeStruct(rhs_cols.shape, F32),...  45.1 us
    unnamed x1, local copies, waits for them, and re-layouts  1.38 us

profile of v3, /device:TPU:1, one launch (start us, length us, event | category | flops | bytes accessed | tf_op | source)
XLA Modules:
  0.0 46.5 jit_solution(12244966371093862795)
XLA Ops:
  0.0 45.1 %shard_map.82 = f32[4,2048]{1,0:T(4,128)} custom-call(f32[3,2048]{1,0:T(4,128)} %points.1, f32[4,2048]{1,0:T(4,128)} %rhs.1, f32[8,8,256]{2,1,0:T(8,128)} %basis_in.1, f32[3,8,64]{2,1,0:T(8,128)} %bitcast.5, f32[8,64,64]{2,1,0:T(8,128)} %lt_in.1, s32[8,9]{1,0:T(8,128)} %mask_in.1, f32[64,64,252]{2,1,0:T(8,128)} %bitcast.3, f32[3,64,254]{2,1,0:T(8,128)} %bitcast.4), custom_call_target="tpu_custom_call" | custom-call | flops 1000000000 | bytes 4000000 | tf_op jit(solution)/shard_map/pallas_call | solution.py:461
  45.1 1.4 %copy.10 = f32[4,2048]{1,0:T(4,128)} copy(f32[4,2048]{1,0:T(4,128)} %shard_map.82) | data formatting | bytes 65536

commit v4 on v3

--- a/solution.py
+++ b/solution.py
@@ -31,7 +31,6 @@
 SLOTS = 9
 EXT = LV + 2 * REACH
 HALO = REACH * LEAF
-AHEAD = 3
 
 
 def split(x):
@@ -95,22 +94,24 @@
         t.nturned[k, 128:256] = jnp.concatenate([x[:, 128:], jnp.zeros((R, 2), F32)], 1).T
 
 
-def operators(t):
-    z, y, c = t.z, t.y, t.c
-
-    def top(n):
-        return t.turned[pl.ds(n, R, stride=256), :]
-
-    t0 = lambda k: top(Y * z + k)
-    t1 = lambda k: top(128 + 4 * z + k)
-    t2 = lambda k: top(192 + 2 * z + k)
-    t3 = lambda k: top(224 + k)
-    t4 = lambda k: top(240 + k)
-    t5 = lambda k: top(248 + k)
+def transfers(t):
+    def at(first):
+        return lambda k: t.turned[pl.ds(first + k, R, stride=256), :]
+
+    return at(Y * t.z), at(128 + 4 * t.z), at(192 + 2 * t.z), at(224), at(240), at(248)
+
+
+def upward(t):
+    t0, t1, t2 = transfers(t)[:3]
     q1 = [mm(t1(k), jnp.concatenate([t0(2 * k), t0(2 * k + 1)], 1), NN) for k in range(4)]
     t.qc[...] = jnp.concatenate(
         [mm(t2(k), jnp.concatenate([q1[2 * k], q1[2 * k + 1]], 1), NN) for k in range(2)], 1
     )
+
+
+def downward(t):
+    z, y, c = t.z, t.y, t.c
+    t0, t1, t2, t3, t4, t5 = transfers(t)
     path = [t0(y), t1(y >> 1), t2(y >> 2), t3(z), t4(z >> 1), t5(z >> 2)]
     e = None
     g_b = []
@@ -159,20 +160,32 @@
 
 
 def leaf_basis_of(t, g):
-    return t.basis[:, g].reshape(R, LEAF)
-
-
-def gather_transfers(t):
-    t.ltc[...] = jnp.concatenate([t.lt[g] for g in range(LV)], 1)
+    return t.basis[:, :, g].reshape(R, LEAF)
+
+
+def turn_transfers(t):
+    for g in range(0, LV, 2):
+        both = jnp.concatenate([t.lt[g], t.lt[g + 1]], 1).T
+        t.ltt[g] = both[0:R].reshape(4, 2, 8, R)
+        t.ltt[g + 1] = both[R : 2 * R].reshape(4, 2, 8, R)
+
+
+def half_root(t):
+    both = jnp.concatenate([t.rh[:, HALO : HALO + LV * LEAF], t.rh_sib[...]], 0)
+    parts = []
+    for g in range(LV):
+        rows = t.basis[:, pl.ds(t.p, 1), g].reshape(R // 2, LEAF)
+        parts.append(mm(both[:, g * LEAF : (g + 1) * LEAF], rows, NT))
+    lifted = mm(jnp.concatenate(parts, 1), t.ltt[:, :, pl.ds(t.p, 1)].reshape(LV * R // 2, R), NN)
+    t.upy[0, t.y] = lifted[0:COLS]
+    t.half[...] = lifted[COLS : 2 * COLS]
 
 
 def expand(t):
     parts = []
     for g in range(LV):
         parts.append(mm(t.rh[:, HALO + g * LEAF : HALO + (g + 1) * LEAF], leaf_basis_of(t, g), NT))
-    moments = jnp.concatenate(parts, 1)
-    t.mom[:, REACH * R : (REACH + LV) * R] = moments
-    t.upy[t.y] = mm(moments, t.ltc[...], NT)
+    t.mom[:, REACH * R : (REACH + LV) * R] = jnp.concatenate(parts, 1)
 
 
 def lift_basis(t):
@@ -280,12 +293,12 @@
 
 
 def level_three(t):
-    flat_y = jnp.concatenate([t.upy[k] for k in range(Y)], 1)
+    flat_y = jnp.concatenate([t.upy[0, k] + t.upy[1, k] for k in range(Y)], 1)
     t.upz[t.z] = mm(flat_y, t.qc[...], NT)
 
 
 def lower_levels(t):
-    flat_y = jnp.concatenate([t.upy[k] for k in range(Y)], 1)
+    flat_y = jnp.concatenate([t.upy[0, k] + t.upy[1, k] for k in range(Y)], 1)
     t.pre[...] = mm(flat_y, t.m0[...].reshape(Y * R, R), NN)
 
 
@@ -307,7 +320,8 @@
     rh=vm(COLS, EXT * LEAF),
     nodes=vm(3, 3, LV, R),
     mom=vm(COLS, EXT * R),
-    basis=vm(8, LV, 8, LEAF),
+    basis=vm(4, 2, LV, 8, LEAF),
+    rh_sib=vm(COLS, LV * LEAF),
     lt=vm(LV, R, R),
     mask=pltpu.VMEM((LV, SLOTS), jnp.int32),
     wn=vm(LV, SLOTS),
@@ -316,11 +330,12 @@
     turned=vm(R * 256, R),
     nslab=vm(3, R, 254),
     nturned=vm(3, 256, R),
-    upy=vm(Y, COLS, R),
+    upy=vm(2, Y, COLS, R),
+    half=vm(COLS, R),
     upz=vm(Z, COLS, R),
     m0=vm(Y, R, R),
     mz=vm(Z, R, R),
-    ltc=vm(R, LV * R),
+    ltt=vm(LV, 4, 2, 8, R),
     qc=vm(R, Y * R),
     wd=vm(R, LV * LEAF),
     pre=vm(COLS, R),
@@ -330,10 +345,11 @@
 DMA = pltpu.SemaphoreType.DMA
 SEMS = dict(
     lsem=DMA((8,)),
-    bs=DMA((2, 7)),
+    bs=DMA((2, 3)),
+    ss=DMA((2, 5)),
     hs=DMA((2, 6)),
     ms=DMA((2, 2)),
-    ys=DMA((2, Y - 1)),
+    ys=DMA((2, 2 * Y - 1)),
     zs=DMA((2, Z - 1)),
     known=pltpu.SemaphoreType.REGULAR((3,)),
 )
@@ -349,24 +365,34 @@
     r = lax.axis_index("rhs")
     z = c // Y
     y = lax.rem(c, Y)
-    t.c, t.z, t.y = c, z, y
+    t.c, t.z, t.y, t.p = c, z, y, lax.rem(r, 2)
+    block = r // 2
+    other = r + 1 - 2 * t.p
     n_clus = Y * Z
     nxt = lax.rem(c + 1, n_clus)
     prv = lax.rem(c + n_clus - 1, n_clus)
 
     r_peers = [(c, lax.rem(r + k, 8)) for k in range(1, 8)]
-    y_at = lambda k: (z * Y + lax.rem(y + Y + k, Y), r)
+    y_at = lambda k, core=r: (z * Y + lax.rem(y + Y + k, Y), core)
     z_at = lambda k: (lax.rem(z + Z + k, Z) * Y + y, r)
+    x_peers = r_peers[1::2]
     y_peers = [y_at(k) for k in range(1, Y)]
+    y_others = [y_at(k, other) for k in range(Y)]
     z_peers = [z_at(k) for k in range(1, Z)]
 
     def signal(sem, p):
         pl.semaphore_signal(sem, inc=1, device_id=p, device_id_type=MESH)
 
-    neighbours = r_peers + [y_at(1), y_at(-1), z_at(1), z_at(-1), (nxt, r), (prv, r)]
+    rank = lax.rem(z + Z - 1, Z)
+    neighbours = r_peers + [y_at(1), y_at(-1), y_at(1, other), y_at(-1, other), (nxt, r), (prv, r)]
     barrier = pltpu.get_barrier_semaphore()
     for p in neighbours:
         signal(barrier, p)
+    for k in range(1, Z):
+
+        @pl.when(rank + k < Z)
+        def _(k=k):
+            signal(barrier, z_at(k))
 
     own = pl.ds(HALO, LV * LEAF)
     loads = [
@@ -377,7 +403,7 @@
         (mask_in, t.mask),
         (lt_in, t.lt),
         (nodes_in, t.nodes.at[1]),
-        (basis_in, t.basis.at[r]),
+        (basis_in, t.basis.at[block, t.p]),
     ]
     local = []
     for i, (src, dst) in enumerate(loads):
@@ -392,9 +418,27 @@
         cp.start()
         return cp
 
-    pl.semaphore_wait(barrier, len(neighbours))
-
-    sent_b = [remote(basis_in, t.basis.at[r], t.bs, i, p) for i, p in enumerate(r_peers)]
+    early = (z == 0) & ((c > 0) | (r > 0))
+
+    def alone():
+        for cp in local:
+            cp.wait()
+        extract(t)
+        upward(t)
+        turn_transfers(t)
+        weights(t)
+
+    @pl.when(early)
+    def _():
+        alone()
+        downward(t)
+
+    pl.semaphore_wait(barrier, len(neighbours) + rank)
+
+    mine = t.basis.at[block, t.p]
+    sent_b = [remote(basis_in, mine, t.bs, i, p) for i, p in enumerate(x_peers)]
+    sent_r = [remote(rhs, t.rh_sib, t.ss, 0, (c, other))]
+    sent_s = [remote(basis_in, mine, t.ss, 1, (c, other))]
     right = pl.ds(LV * LEAF - HALO, HALO)
     left = pl.ds(0, HALO)
     to_left = pl.ds(0, HALO)
@@ -407,25 +451,46 @@
         remote(nodes_in, t.nodes.at[0], t.hs, 4, (nxt, r)),
         remote(nodes_in, t.nodes.at[2], t.hs, 5, (prv, r)),
     ]
-    for p in (y_at(1), y_at(-1), z_at(1), z_at(-1)):
+    for p in (y_at(1), y_at(-1)):
         signal(t.known.at[0], p)
-    for cp in local:
-        cp.wait()
-    extract(t)
-    pl.semaphore_wait(t.known.at[0], 4)
-    for p in (y_at(2), y_at(-2), z_at(2), z_at(-2)):
+    for k in range(1, Z):
+
+        @pl.when(rank - k >= 0)
+        def _(k=k):
+            signal(t.known.at[2], z_at(-k))
+
+    @pl.when(jnp.logical_not(early))
+    def _():
+        alone()
+
+    pl.semaphore_wait(t.known.at[0], 2)
+    for p in (y_at(2), y_at(-2)):
         signal(t.known.at[1], p)
-    operators(t)
-    pl.semaphore_wait(t.known.at[1], 4)
-    for p in (z_at(4), z_at(-4)):
-        signal(t.known.at[2], p)
-    gather_transfers(t)
-    weights(t)
-
-    for cp in sent_b:
+    for cp in sent_h:
+        cp.wait_recv()
+    ready = jnp.where(early, EXT, 0)
+    first = jnp.where(early, 1, 0)
+    second = jnp.where(early, 5, 0)
+    sources(t, 0, ready)
+    near(t, 0, first)
+    pl.semaphore_wait(t.known.at[1], 2)
+
+    for cp in sent_b + sent_r:
+        cp.wait_recv()
+    half_root(t)
+    sent_y = [remote(t.upy.at[0, y], t.upy.at[0, y], t.ys, i, p) for i, p in enumerate(y_peers)]
+    sent_y += [remote(t.half, t.upy.at[1, y], t.ys, Y - 1 + i, p) for i, p in enumerate(y_others)]
+    for k in range(1, 4):
+        there = t.basis.at[lax.rem(block + k, 4), t.p]
+        sent_s.append(remote(there, there, t.ss, 1 + k, (c, other)))
+
+    @pl.when(jnp.logical_not(early))
+    def _():
+        downward(t)
+
+    for cp in sent_s:
         cp.wait_recv()
     expand(t)
-    sent_y = [remote(t.upy.at[y], t.upy.at[y], t.ys, i, p) for i, p in enumerate(y_peers)]
     out_r = pl.ds(LV * R, REACH * R)
     out_l = pl.ds(REACH * R, REACH * R)
     sent_m = [
@@ -433,18 +498,20 @@
         remote(t.mom.at[:, out_l], t.mom.at[:, pl.ds((REACH + LV) * R, REACH * R)], t.ms, 1, (prv, r)),
     ]
     lift_basis(t)
-    for cp in sent_h:
-        cp.wait_recv()
-    sources(t, 0, EXT)
-    near(t, 0, AHEAD)
-
-    pl.semaphore_wait(t.known.at[2], 2)
+    sources(t, ready, EXT - ready)
+    near(t, first, second - first)
+
+
+    @pl.when(rank < Z - 1)
+    def _():
+        pl.semaphore_wait(t.known.at[2], Z - 1 - rank)
+
     for cp in sent_y:
         cp.wait_recv()
     level_three(t)
     sent_z = [remote(t.upz.at[z], t.upz.at[z], t.zs, i, p) for i, p in enumerate(z_peers)]
     lower_levels(t)
-    near(t, AHEAD, LV - AHEAD)
+    near(t, second, LV - second)
     for cp in sent_m:
         cp.wait_recv()
     leaf_far(t)
@@ -452,7 +519,7 @@
     for cp in sent_z:
         cp.wait_recv()
     finish(t)
-    for cp in sent_b + sent_h + sent_m + sent_y + sent_z:
+    for cp in sent_b + sent_r + sent_s + sent_h + sent_m + sent_y + sent_z:
         cp.wait_send()
 
 

time: 46.7 us -> 43.2 us (0.925)
  Pallas kernels: 45.1 us -> 41.3 us
    pallas_call x1, Pallas kernels: 45.1 us -> 41.3 us  [on_device(): pl.pallas_call(body, out_shape=jax.ShapeDtypeStruct(rhs_cols.shape, F32),...]
where the time goes in v4:
time: 43.2 us; the launch traced here: 42.7 us
  Pallas kernels  41.3 us (96%)
  local copies, waits for them, and re-layouts  1.38 us (3%)
    pallas_call x1, Pallas kernels, on_device(): pl.pallas_call(body, out_shape=jax.ShapeDtypeStruct(rhs_cols.shape, F32),...  41.3 us
    unnamed x1, local copies, waits for them, and re-layouts  1.38 us

profile of v4, /device:TPU:1, one launch (start us, length us, event | category | flops | bytes accessed | tf_op | source)
XLA Modules:
  0.0 42.7 jit_solution(6811265127425599726)
XLA Ops:
  0.0 41.3 %shard_map.82 = f32[4,2048]{1,0:T(4,128)} custom-call(f32[3,2048]{1,0:T(4,128)} %points.1, f32[4,2048]{1,0:T(4,128)} %rhs.1, f32[8,8,256]{2,1,0:T(8,128)} %basis_in.1, f32[3,8,64]{2,1,0:T(8,128)} %bitcast.5, f32[8,64,64]{2,1,0:T(8,128)} %lt_in.1, s32[8,9]{1,0:T(8,128)} %mask_in.1, f32[64,64,252]{2,1,0:T(8,128)} %bitcast.3, f32[3,64,254]{2,1,0:T(8,128)} %bitcast.4), custom_call_target="tpu_custom_call" | custom-call | flops 1000000000 | bytes 4000000 | tf_op jit(solution)/shard_map/pallas_call | solution.py:528
  41.3 1.4 %copy.10 = f32[4,2048]{1,0:T(4,128)} copy(f32[4,2048]{1,0:T(4,128)} %shard_map.82) | data formatting | bytes 65536

commit v5 on v4

--- a/solution.py
+++ b/solution.py
@@ -351,7 +351,7 @@
     ms=DMA((2, 2)),
     ys=DMA((2, 2 * Y - 1)),
     zs=DMA((2, Z - 1)),
-    known=pltpu.SemaphoreType.REGULAR((3,)),
+    known=pltpu.SemaphoreType.REGULAR((2,)),
 )
 
 
@@ -383,8 +383,9 @@
     def signal(sem, p):
         pl.semaphore_signal(sem, inc=1, device_id=p, device_id_type=MESH)
 
-    rank = lax.rem(z + Z - 1, Z)
-    neighbours = r_peers + [y_at(1), y_at(-1), y_at(1, other), y_at(-1, other), (nxt, r), (prv, r)]
+    rank = jnp.where((y == 0) & (r == 0), lax.rem(z + Z - 1, Z), z)
+    neighbours = r_peers + [y_at(k, q) for k in (1, -1, 2, -2) for q in (r, other)]
+    neighbours += [(nxt, r), (prv, r)]
     barrier = pltpu.get_barrier_semaphore()
     for p in neighbours:
         signal(barrier, p)
@@ -451,29 +452,26 @@
         remote(nodes_in, t.nodes.at[0], t.hs, 4, (nxt, r)),
         remote(nodes_in, t.nodes.at[2], t.hs, 5, (prv, r)),
     ]
-    for p in (y_at(1), y_at(-1)):
+    for p in (y_at(2), y_at(-2)):
         signal(t.known.at[0], p)
     for k in range(1, Z):
 
         @pl.when(rank - k >= 0)
         def _(k=k):
-            signal(t.known.at[2], z_at(-k))
+            signal(t.known.at[1], z_at(-k))
 
     @pl.when(jnp.logical_not(early))
     def _():
         alone()
 
-    pl.semaphore_wait(t.known.at[0], 2)
-    for p in (y_at(2), y_at(-2)):
-        signal(t.known.at[1], p)
     for cp in sent_h:
         cp.wait_recv()
     ready = jnp.where(early, EXT, 0)
     first = jnp.where(early, 1, 0)
-    second = jnp.where(early, 5, 0)
+    second = jnp.where(early, 6, 0)
     sources(t, 0, ready)
     near(t, 0, first)
-    pl.semaphore_wait(t.known.at[1], 2)
+    pl.semaphore_wait(t.known.at[0], 2)
 
     for cp in sent_b + sent_r:
         cp.wait_recv()
@@ -498,19 +496,21 @@
         remote(t.mom.at[:, out_l], t.mom.at[:, pl.ds((REACH + LV) * R, REACH * R)], t.ms, 1, (prv, r)),
     ]
     lift_basis(t)
-    sources(t, ready, EXT - ready)
+    middle = jnp.where(z < 4, EXT, 0)
+    sources(t, ready, middle - ready)
     near(t, first, second - first)
 
 
     @pl.when(rank < Z - 1)
     def _():
-        pl.semaphore_wait(t.known.at[2], Z - 1 - rank)
+        pl.semaphore_wait(t.known.at[1], Z - 1 - rank)
 
     for cp in sent_y:
         cp.wait_recv()
     level_three(t)
     sent_z = [remote(t.upz.at[z], t.upz.at[z], t.zs, i, p) for i, p in enumerate(z_peers)]
     lower_levels(t)
+    sources(t, middle, EXT - middle)
     near(t, second, LV - second)
     for cp in sent_m:
         cp.wait_recv()

time: 43.2 us -> 43 us (level)
  no operation moved by 1% of the time
where the time goes in v5:
time: 43 us; the launch traced here: 42.7 us
  Pallas kernels  41.3 us (96%)
  local copies, waits for them, and re-layouts  1.38 us (3%)
    pallas_call x1, Pallas kernels, on_device(): pl.pallas_call(body, out_shape=jax.ShapeDtypeStruct(rhs_cols.shape, F32),...  41.3 us
    unnamed x1, local copies, waits for them, and re-layouts  1.38 us

profile of v5, /device:TPU:1, one launch (start us, length us, event | category | flops | bytes accessed | tf_op | source)
XLA Modules:
  0.0 42.7 jit_solution(18320329910892491909)
XLA Ops:
  0.0 41.3 %shard_map.82 = f32[4,2048]{1,0:T(4,128)} custom-call(f32[3,2048]{1,0:T(4,128)} %points.1, f32[4,2048]{1,0:T(4,128)} %rhs.1, f32[8,8,256]{2,1,0:T(8,128)} %basis_in.1, f32[3,8,64]{2,1,0:T(8,128)} %bitcast.5, f32[8,64,64]{2,1,0:T(8,128)} %lt_in.1, s32[8,9]{1,0:T(8,128)} %mask_in.1, f32[64,64,252]{2,1,0:T(8,128)} %bitcast.3, f32[3,64,254]{2,1,0:T(8,128)} %bitcast.4), custom_call_target="tpu_custom_call" | custom-call | flops 1000000000 | bytes 4000000 | tf_op jit(solution)/shard_map/pallas_call | solution.py:528
  41.3 1.4 %copy.10 = f32[4,2048]{1,0:T(4,128)} copy(f32[4,2048]{1,0:T(4,128)} %shard_map.82) | data formatting | bytes 65536
